TPU v7x, 512 devices: a whole 4x4x16 slice. The times are simulated.
512 devices in a mesh: pulse: 64 (over z, x), range: 8 (over y, core).
Axes of the slice: x: 4, y: 4, z: 16, core: 2. Of those that a mesh axis runs over, the one named last changes fastest.
Arguments:
- echo: bfloat16 [128, 2, 32768], P('pulse', None, 'range'), may hold values from -6 to 6
- chirp_phase: float32 [256], replicated, may hold values from -0.5 to 201.5624
- rec_phase: float32 [8, 8192, 2], P('range', 'pulse'), may hold values from -3.140625 to 3.140625
- rec_start: int32 [8, 8192], P('range', 'pulse'), may hold values from 0 to 32256
- rec_owner: int32 [8, 8192, 1], P('range', 'pulse'), may hold values from 0 to 511; in each aligned block of 128 rows (0 to 127, 128 to 255, ..., all dimensions but the last counted through in order) at most 2 rows name the same one
- rec_row: int32 [8, 8192], P('range', 'pulse'), may hold values from 0 to 63
- rec_weight: float32 [8, 8192], P('range', 'pulse'), may hold values from 0.2 to 1
- rec_count: int32 [8, 64], P('range', 'pulse'), may hold values from 96 to 128, as said below
- prior: bfloat16 [2048, 2, 4096], P('pulse', None, 'range'), may hold values from -6 to 6
- interp_weight: bfloat16 [64, 32], replicated, may hold values from -1 to 1
Outputs:
- tiles: float32 [4096, 2, 4096], P('pulse', None, 'range')
Inputs may be any that keep to these rules, and one draw needn't show every extreme that they name: `rec_owner`: in each aligned block of 128 record slots (one device's slots) no owner is named more than 2 times. Owner o is the tile of pulse index o // 8 and range index o % 8, 8 being the number of range devices. `rec_count`: some subimage has all 128 slots live.
All inputs are finite; a program needn't handle non-finite values.
Results may differ from a plain program's by a relative error of at most 0.0034.
Values may be sent and summed in bfloat16 or wider, within the bound.
A program may use at most 64 MiB of HBM per device.

v0:
```python
import jax
import jax.numpy as jnp
from jax import lax
from jax.sharding import PartitionSpec as P

SEG = 512


def shifted(block, axis, distance):
    devices = range(lax.axis_size(axis))
    route = [(i - distance, i) for i in devices if i - distance in devices]
    return lax.ppermute(block, axis, route)


def chirp_matrix(chirp_phase):
    tap_count = chirp_phase.shape[0]
    tap_scale = 1.0 / jnp.sqrt(jnp.float32(tap_count))
    real_taps = jnp.cos(chirp_phase) * tap_scale
    imag_taps = jnp.sin(chirp_phase) * tap_scale

    def banded(values):
        padded = jnp.concatenate([values, jnp.zeros((tap_count + 1,), jnp.float32)])
        return (
            jnp.tile(padded, tap_count)[: 2 * tap_count * tap_count]
            .reshape(tap_count, 2 * tap_count)
            .T
        )

    real_band = banded(real_taps)
    imag_band = banded(imag_taps)
    upper = jnp.concatenate([real_band, -imag_band], axis=1)
    lower = jnp.concatenate([imag_band, real_band], axis=1)
    return jnp.concatenate([upper, lower], axis=0).astype(jnp.bfloat16)


def compress(echo_block, tail_rim, filter_matrix):
    pulses, planes, bin_count = echo_block.shape
    tap_count = filter_matrix.shape[1] // 2
    block_count = bin_count // tap_count
    extended = jnp.concatenate([echo_block, tail_rim], axis=2)
    left_half = extended[:, :, :bin_count].reshape(pulses, planes, block_count, tap_count)
    right_half = extended[:, :, tap_count:].reshape(pulses, planes, block_count, tap_count)
    windows = jnp.concatenate([left_half, right_half], axis=3)
    windows = windows.transpose(0, 2, 1, 3).reshape(pulses * block_count, 2 * planes * tap_count)
    filtered = jnp.dot(windows, filter_matrix, preferred_element_type=jnp.float32)
    filtered = filtered.reshape(pulses, block_count, planes, tap_count).transpose(0, 2, 1, 3)
    return filtered.reshape(pulses, planes, bin_count).astype(jnp.bfloat16)


def cut_windows(block_table, starts):
    block_total = block_table.shape[0]
    first_block = starts // SEG
    second_block = jnp.minimum(first_block + 1, block_total - 1)
    offsets = starts % SEG
    paired = jnp.concatenate([block_table[first_block], block_table[second_block]], axis=3)
    for bit_number in range((SEG - 1).bit_length()):
        step_size = 1 << bit_number
        moved = jnp.concatenate(
            [paired[..., step_size:], jnp.zeros(paired.shape[:-1] + (step_size,), paired.dtype)],
            axis=3,
        )
        chosen = (offsets // step_size % 2 == 1)[:, None, None, None]
        paired = jnp.where(chosen, moved, paired)
    return paired[..., :SEG]


def form_records(block_table, starts, phases, scales):
    windows = cut_windows(block_table, starts)
    cosine = jnp.cos(phases).astype(jnp.bfloat16)
    sine_part = jnp.sin(phases).astype(jnp.bfloat16)
    real_part = windows[:, :, 0]
    imag_part = windows[:, :, 1]
    out_real = jnp.einsum(
        "bk,bks->bs", cosine, real_part, preferred_element_type=jnp.float32
    ) - jnp.einsum("bk,bks->bs", sine_part, imag_part, preferred_element_type=jnp.float32)
    out_imag = jnp.einsum(
        "bk,bks->bs", cosine, imag_part, preferred_element_type=jnp.float32
    ) + jnp.einsum("bk,bks->bs", sine_part, real_part, preferred_element_type=jnp.float32)
    return (jnp.stack([out_real, out_imag], axis=1) * scales[:, None, None]).astype(jnp.bfloat16)


def on_device(
    echo,
    chirp_phase,
    rec_phase,
    rec_start,
    rec_owner,
    rec_row,
    rec_weight,
    rec_count,
    prior,
    interp_weight,
):
    filter_matrix = chirp_matrix(chirp_phase)
    tap_count = chirp_phase.shape[0]
    tail_rim = shifted(echo[:, :, :tap_count], "range", -1)
    profiles = lax.all_gather(compress(echo, tail_rim, filter_matrix), "range", axis=2, tiled=True)
    pulses, planes, bin_total = profiles.shape
    block_table = profiles.reshape(pulses, planes, bin_total // SEG, SEG).transpose(2, 0, 1, 3)
    slot_count = rec_start.shape[1]
    starts = rec_start[0]
    phases = rec_phase[0]
    owners = rec_owner[0, :, 0]
    dest_rows = rec_row[0]
    weights = rec_weight[0]
    live_mask = (jnp.arange(slot_count) < rec_count[0, 0]).astype(jnp.float32)
    scales = live_mask * weights / jnp.sqrt(jnp.float32(pulses))
    block_size = min(64, slot_count)
    group_count = slot_count // block_size

    def form_group(items):
        return form_records(block_table, items[0], items[1], items[2])

    records = lax.map(
        form_group,
        (
            starts.reshape(group_count, block_size),
            phases.reshape(group_count, block_size, pulses),
            scales.reshape(group_count, block_size),
        ),
    )
    records = records.reshape(slot_count, 2 * SEG)
    pulse_count = lax.axis_size("pulse")
    range_count = lax.axis_size("range")
    owner_total = pulse_count * range_count
    capacity = max(2, 3 * slot_count // (2 * owner_total))
    owner_marks = (owners[:, None] == jnp.arange(owner_total)[None, :]).astype(jnp.int32)
    earlier = jnp.cumsum(owner_marks, axis=0) - owner_marks
    slot_rank = jnp.sum(earlier * owner_marks, axis=1)
    slot_index = owners * capacity + slot_rank
    placement = slot_index[None, :] == jnp.arange(owner_total * capacity)[:, None]
    outgoing = jnp.dot(
        placement.astype(jnp.bfloat16), records, preferred_element_type=jnp.float32
    ).astype(jnp.bfloat16)
    row_slots = jnp.sum(placement.astype(jnp.int32) * dest_rows[None, :], axis=1)
    outgoing = outgoing.reshape(pulse_count, range_count, capacity, 2, SEG)
    row_slots = row_slots.reshape(pulse_count, range_count, capacity)
    incoming, incoming_rows = (
        lax.all_to_all(
            lax.all_to_all(outgoing, "pulse", split_axis=0, concat_axis=0, tiled=True),
            "range",
            split_axis=1,
            concat_axis=1,
            tiled=True,
        ),
        lax.all_to_all(
            lax.all_to_all(row_slots, "pulse", split_axis=0, concat_axis=0, tiled=True),
            "range",
            split_axis=1,
            concat_axis=1,
            tiled=True,
        ),
    )
    incoming = incoming.reshape(-1, 2, SEG)
    incoming_rows = incoming_rows.reshape(-1)
    out_rows = interp_weight.shape[0]
    tile_image = jnp.einsum("rm,mcs->rcs", interp_weight, prior, preferred_element_type=jnp.float32)
    row_table = (incoming_rows[:, None] == jnp.arange(out_rows)[None, :]).astype(jnp.bfloat16)
    tile_image = tile_image + jnp.einsum(
        "jr,jcs->rcs", row_table, incoming, preferred_element_type=jnp.float32
    )
    return tile_image


def solution(mesh):
    placed = (
        P("pulse", None, "range"),
        P(),
        P("range", "pulse", None),
        P("range", "pulse"),
        P("range", "pulse", None),
        P("range", "pulse"),
        P("range", "pulse"),
        P("range", "pulse"),
        P("pulse", None, "range"),
        P(),
    )
    return jax.shard_map(
        on_device, mesh=mesh, in_specs=placed, out_specs=P("pulse", None, "range"), check_vma=False
    )
```

profile of v0, /device:TPU:1, one launch (start us, length us, event | category | flops | bytes accessed | tf_op | source)
XLA Modules:
  0.0 257.0 jit_solution(12730651310429651620)
XLA Ops:
  0.0 0.7 slice.92
  0.7 8.8 %collective-permute-start = (bf16[2,2,256]{2,1,0:T(2,128)(2,1)S(1)}, bf16[2,2,256]{2,1,0:T(2,128)(2,1)S(1)}, u32[]{:S(2)}, u32[]{:S(2)}) collective-permute-start(bf16[2,2,256]{2,1,0:T(2,128)(2,1)S(1)} %slice.92), channel_id=1, source_target_pairs={{1,0},{2,1},{3,2},{4,3},{5,4},{6,5},{7,6},{9,8},{10,9},{11,10},{12... | collective-permute-start | bytes 6152 | tf_op jit(solution)/shard_map/ppermute | solution.py:12
  9.5 0.7 fusion.35
  10.5 0.9 select_reduce_fusion.1
  11.4 0.7 multiply_add_fusion
  12.0 0.9 select_reduce_fusion
  13.1 1.1 copy.61
  14.2 12.9 %all-to-all-start = ((s32[64,8,2]{1,2,0:T(2,128)}), s32[64,8,2]{1,2,0:T(2,128)S(1)}, u32[]{:S(2)}, u32[]{:S(2)}) async-start(s32[64,8,2]{1,2,0:T(2,128)} %copy.61), calls=%async_computation | async-start | bytes 131072 | tf_op jit(solution)/shard_map/all_to_all | solution.py:147
  27.1 0.7 sine_multiply_fusion
  29.0 0.6 tile.9
  31.8 0.6 broadcast.1368
  32.4 0.7 reduce.6
  33.8 13.5 %all_gather.3 = bf16[2,2,32768]{2,1,0:T(2,128)(2,1)S(1)} all-gather(bf16[2,2,4096]{2,1,0:T(2,128)(2,1)S(1)} %convert_element_type.57), channel_id=1, replica_groups=mesh['pulse'=64,'range'=8] {'range'}, dimensions={2}, use_global_device_ids=true | all-gather | bytes 294912 | tf_op jit(solution)/shard_map/all_gather | solution.py:97
  47.8 42.9 %while.13 = (s32[]{:T(128)}, bf16[2,64,2,512]{3,2,1,0:T(2,128)(2,1)S(1)}, f32[2,64,2]{1,0,2:T(2,128)S(1)}, s32[2,64]{1,0:T(2,128)S(1)}, bf16[64,2,2,512]{3,2,1,0...) while((s32[]{:T(128)}, bf16[2,64,2,512]{3,2,1,0:T(2,128)(2,1)S(1)}, f32[2,64,2]{1,0,2:T(2,128)S(1)}, ...), condition=%wide.region_4.5_spmd, body=%wide.region_3.4_spmd.sunk | while | flops 3162434 | bytes 28723936 | solution.py:114
  48.0 1.1 gather_fusion
  49.3 1.1 gather_fusion.1
  50.6 1.0 slice.137
  51.7 1.0 broadcast_select_fusion.18
  52.7 1.0 slice.138
  53.7 1.0 broadcast_select_fusion.19
  54.7 1.0 slice.139
  55.7 1.0 broadcast_select_fusion.20
  56.7 1.0 slice.140
  57.7 1.0 broadcast_select_fusion.21
  58.7 1.0 slice.141
  59.7 1.0 broadcast_select_fusion.22
  60.7 1.0 slice.142
  61.7 1.0 broadcast_select_fusion.23
  62.7 1.0 slice.143
  63.7 1.0 broadcast_select_fusion.24
  65.0 0.7 broadcast_select_fusion.25
  66.0 0.7 broadcast_select_fusion.26
  69.3 1.1 gather_fusion
  70.5 1.1 gather_fusion.1
  71.9 1.0 slice.137
  72.9 1.0 broadcast_select_fusion.18
  73.9 1.0 slice.138
  74.9 1.0 broadcast_select_fusion.19
  75.9 1.0 slice.139
  76.9 1.0 broadcast_select_fusion.20
  77.9 1.0 slice.140
  78.9 1.0 broadcast_select_fusion.21
  79.9 1.0 slice.141
  80.9 1.0 broadcast_select_fusion.22
  81.9 1.0 slice.142
  82.9 1.0 broadcast_select_fusion.23
  83.9 1.0 slice.143
  84.9 1.0 broadcast_select_fusion.24
  86.2 0.7 broadcast_select_fusion.25
  87.2 0.7 broadcast_select_fusion.26
  90.7 0.7 convolution_convert_fusion
  91.4 2.7 %reshape.460 = bf16[64,8,2,2,512]{4,3,2,1,0:T(2,128)(2,1)} reshape(bf16[1024,1024]{1,0:T(8,128)(2,1)S(1)} %convolution_convert_fusion) | data formatting | bytes 4194304 | tf_op jit(solution)/shard_map/reshape | solution.py:136
  94.1 14.8 %all-to-all-start.2 = ((bf16[64,8,2,2,512]{4,3,2,1,0:T(2,128)(2,1)}), bf16[64,8,2,2,512]{4,3,2,1,0:T(2,128)(2,1)S(1)}, u32[]{:S(2)}, u32[]{:S(2)}) async-start(bf16[64,8,2,2,512]{4,3,2,1,0:T(2,128)(2,1)} %reshape.460), calls=%async_computation.2 | async-start | bytes 4194304 | tf_op jit(solution)/shard_map/all_to_all | solution.py:140
  109.0 0.7 reshape.511
  109.7 96.3 %all-to-all-done.2 = bf16[64,8,2,2,512]{4,3,2,1,0:T(2,128)(2,1)S(1)} async-done(((bf16[64,8,2,2,512]{4,3,2,1,0:T(2,128)(2,1)}), bf16[64,8,2,2,512]{4,3,2,1,0:T(2,128)(2,1)S(1)}, u32[]{:S(2)}, u32[]{:S(2)}) %all-to-all-start.2) | async-done | bytes 2097184 | tf_op jit(solution)/shard_map/all_to_all | solution.py:140
  206.0 8.1 %all-to-all-start.1 = ((s32[8,1,128]{2,1,0:T(1,128)}), s32[8,1,128]{2,1,0:T(1,128)S(1)}, u32[]{:S(2)}, u32[]{:S(2)}) async-start(s32[8,1,128]{2,1,0:T(1,128)} %reshape.511), calls=%async_computation.1 | async-start | bytes 8192 | tf_op jit(solution)/shard_map/all_to_all | solution.py:146
  214.1 3.0 %copy.68 = bf16[64,8,2,2,512]{4,3,2,0,1:T(2,128)(2,1)} copy(bf16[64,8,2,2,512]{4,3,2,1,0:T(2,128)(2,1)S(1)} %all-to-all-done.2) | data formatting | bytes 4194304 | tf_op jit(solution)/shard_map/all_to_all | solution.py:140
  217.0 1.5 all-to-all-done.1
  218.6 4.2 %all-to-all-start.3 = ((bf16[64,8,2,2,512]{4,3,2,0,1:T(2,128)(2,1)}), bf16[64,8,2,2,512]{4,3,2,0,1:T(2,128)(2,1)S(1)}, u32[]{:S(2)}, u32[]{:S(2)}) async-start(bf16[64,8,2,2,512]{4,3,2,0,1:T(2,128)(2,1)} %copy.68), calls=%async_computation.3 | async-start | bytes 4194304 | tf_op jit(solution)/shard_map/all_to_all | solution.py:139
  223.5 0.7 reduce.8
  224.6 24.5 %all-to-all-done.3 = bf16[64,8,2,2,512]{4,3,2,0,1:T(2,128)(2,1)S(1)} async-done(((bf16[64,8,2,2,512]{4,3,2,0,1:T(2,128)(2,1)}), bf16[64,8,2,2,512]{4,3,2,0,1:T(2,128)(2,1)S(1)}, u32[]{:S(2)}, u32[]{:S(2)}) %all-to-all-start.3) | async-done | bytes 2097184 | tf_op jit(solution)/shard_map/all_to_all | solution.py:139
  249.1 3.8 %copy.69 = bf16[64,8,2,2,512]{4,2,1,0,3:T(2,128)(2,1)} copy(bf16[64,8,2,2,512]{4,3,2,0,1:T(2,128)(2,1)S(1)} %all-to-all-done.3) | data formatting | bytes 4194304 | tf_op jit(solution)/shard_map/all_to_all | solution.py:139
  252.9 2.7 %reshape.461 = bf16[1024,2,512]{2,0,1:T(8,128)(2,1)S(1)} reshape(bf16[64,8,2,2,512]{4,2,1,0,3:T(2,128)(2,1)} %copy.69) | data formatting | bytes 4194304 | tf_op jit(solution)/shard_map/reshape | solution.py:154
  256.1 0.9 copy.70
  (105 shorter events, 12.9 us)
Async XLA Ops:
  0.0 222.8 %copy-start = (bf16[32,2,512]{2,1,0:T(2,128)(2,1)S(1)}, bf16[32,2,512]{2,1,0:T(2,128)(2,1)}, u32[]{:S(2)}) copy-start(bf16[32,2,512]{2,1,0:T(2,128)(2,1)} %param.20) | copy-start | bytes 196612
  0.7 32.5 %collective-permute-start = (bf16[2,2,256]{2,1,0:T(2,128)(2,1)S(1)}, bf16[2,2,256]{2,1,0:T(2,128)(2,1)S(1)}, u32[]{:S(2)}, u32[]{:S(2)}) collective-permute-start(bf16[2,2,256]{2,1,0:T(2,128)(2,1)S(1)} %slice.92), channel_id=1, source_target_pairs={{1,0},{2,1},{3,2},{4,3},{5,4},{6,5},{7,6},{9,8},{10,9},{11,10},{12... | collective-permute-start | bytes 6152 | tf_op jit(solution)/shard_map/ppermute | solution.py:12
  10.5 18.0 %copy-start.4 = (f32[256]{0:T(256)S(1)}, f32[256]{0:T(256)}, u32[]{:S(2)}) copy-start(f32[256]{0:T(256)} %param.13) | copy-start | bytes 3076
  14.2 80.0 %all-to-all-start = ((s32[64,8,2]{1,2,0:T(2,128)}), s32[64,8,2]{1,2,0:T(2,128)S(1)}, u32[]{:S(2)}, u32[]{:S(2)}) async-start(s32[64,8,2]{1,2,0:T(2,128)} %copy.61), calls=%async_computation | async-start | bytes 131072 | tf_op jit(solution)/shard_map/all_to_all | solution.py:147
  28.4 1.9 copy-start.5
  28.7 3.1 %copy-start.3 = (f32[1,128,2]{1,2,0:T(2,128)S(1)}, f32[1,128,2]{1,2,0:T(2,128)}, u32[]{:S(2)}) copy-start(f32[1,128,2]{1,2,0:T(2,128)} %param.14) | copy-start | bytes 3076
  28.7 3.7 %copy-start.6 = (s32[1,128]{1,0:T(1,128)S(1)}, s32[1,128]{1,0:T(1,128)}, u32[]{:S(2)}) copy-start(s32[1,128]{1,0:T(1,128)} %param.15) | copy-start | bytes 1540
  28.7 4.5 %copy-start.1 = (bf16[2,2,4096]{2,1,0:T(2,128)(2,1)S(1)}, bf16[2,2,4096]{2,1,0:T(2,128)(2,1)}, u32[]{:S(2)}) copy-start(bf16[2,2,4096]{2,1,0:T(2,128)(2,1)} %param.12) | copy-start | bytes 98308
  94.1 111.8 %all-to-all-start.2 = ((bf16[64,8,2,2,512]{4,3,2,1,0:T(2,128)(2,1)}), bf16[64,8,2,2,512]{4,3,2,1,0:T(2,128)(2,1)S(1)}, u32[]{:S(2)}, u32[]{:S(2)}) async-start(bf16[64,8,2,2,512]{4,3,2,1,0:T(2,128)(2,1)} %reshape.460), calls=%async_computation.2 | async-start | bytes 4194304 | tf_op jit(solution)/shard_map/all_to_all | solution.py:140
  206.0 12.6 %all-to-all-start.1 = ((s32[8,1,128]{2,1,0:T(1,128)}), s32[8,1,128]{2,1,0:T(1,128)S(1)}, u32[]{:S(2)}, u32[]{:S(2)}) async-start(s32[8,1,128]{2,1,0:T(1,128)} %reshape.511), calls=%async_computation.1 | async-start | bytes 8192 | tf_op jit(solution)/shard_map/all_to_all | solution.py:146
  217.0 5.7 %copy-start.2 = (bf16[64,32]{0,1:T(8,128)(2,1)S(1)}, bf16[64,32]{0,1:T(8,128)(2,1)}, u32[]{:S(2)}) copy-start(bf16[64,32]{0,1:T(8,128)(2,1)} %param.21) | copy-start | bytes 12292
  218.6 30.6 %all-to-all-start.3 = ((bf16[64,8,2,2,512]{4,3,2,0,1:T(2,128)(2,1)}), bf16[64,8,2,2,512]{4,3,2,0,1:T(2,128)(2,1)S(1)}, u32[]{:S(2)}, u32[]{:S(2)}) async-start(bf16[64,8,2,2,512]{4,3,2,0,1:T(2,128)(2,1)} %copy.68), calls=%async_computation.3 | async-start | bytes 4194304 | tf_op jit(solution)/shard_map/all_to_all | solution.py:139
where the time goes:
time: 258 us; the launch traced here: 257 us
  waiting for transfers between devices  122 us (47%)
  starting transfers between devices  48.8 us (19%)
  local copies, waits for them, and re-layouts  42.8 us (17%)
  other arithmetic  23.8 us (9%)
  blocking collectives  13.5 us (5%)
  matrix products  3.97 us (2%)
    all_to_all x1, waiting for transfers between devices, on_device(): lax.all_to_all(outgoing, 'pulse', split_axis=0, concat_axis=0, tiled=True)  96.3 us
    all_to_all x1, waiting for transfers between devices, on_device(): lax.all_to_all(lax.all_to_all(outgoing, 'pulse', split_axis=0, concat_axi...  24.5 us
    select_n x18, other arithmetic, cut_windows(): paired = jnp.where(chosen, moved, paired)  16.4 us
    slice x18, local copies, waits for them, and re-layouts, cut_windows(): paired[..., step_size:]  15.4 us
    all_to_all x1, starting transfers between devices, on_device(): lax.all_to_all(outgoing, 'pulse', split_axis=0, concat_axis=0, tiled=True)  14.8 us
    all_gather x1, blocking collectives, on_device(): lax.all_gather(compress(echo, tail_rim, filter_matrix), 'range', axis=2,...  13.5 us
    all_to_all x1, starting transfers between devices, on_device(): lax.all_to_all(row_slots, 'pulse', split_axis=0, concat_axis=0, tiled=True)  12.9 us
    ppermute x1, starting transfers between devices, shifted(): return lax.ppermute(block, axis, route)  8.77 us
  transfers between devices with their start and end apart: 5, of which 3 were waited for; matrix products, arithmetic and copies ran while one was open for 24% of the time, Pallas kernels for 0%

commit v1 on v0

v1 whole, which is shorter than its diff:
```python
import functools

import jax
import jax.numpy as jnp
from jax import lax
from jax.experimental import pallas as pl
from jax.experimental.pallas import tpu as pltpu
from jax.sharding import PartitionSpec as P

MESH = pl.DeviceIdType.MESH
LANES = 128
NT = (((1,), (1,)), ((), ()))


def position():
    pulse, rng = lax.axis_index("pulse"), lax.axis_index("range")
    return pulse // 4, lax.rem(pulse, 4), rng // 2, lax.rem(rng, 2)


def at(z, x, y, c):
    return (lax.rem(z + 16, 16) * 4 + lax.rem(x + 4, 4), lax.rem(y + 4, 4) * 2 + c)


def swap_planes(rows):
    count = rows.shape[0]
    even = lax.rem(lax.broadcasted_iota(jnp.int32, rows.shape, 0), 2) == 0
    return jnp.where(even, pltpu.roll(rows, count - 1, 0), -pltpu.roll(rows, 1, 0))


def gather_kernel(
    echo_ref, tap_cos_ref, tap_sin_ref, cos_ref, sin_ref, start_ref, owner_ref, owner_col_ref,
    row_ref, weight_ref, count_ref,
    prof_ref, meta_ref,
    ext, halo, own, own_meta, local_sem,
    halo_s, halo_r, z_s, z_r, mz_s, mz_r, a_s, a_r, b_s, b_r, t_s, t_r,
):
    z, x, y, c = position()
    twin = at(z, x, y, 1 - c)
    rng = y * 2 + c
    before = (lax.axis_index("pulse"), lax.rem(rng + 7, 8))
    after = (lax.axis_index("pulse"), lax.rem(rng + 1, 8))
    barrier = pltpu.get_barrier_semaphore()
    partners = [twin, before, after]
    for d in (1, 2, 3):
        partners += [at(z + 4 * d, x, y, c), at(z, x + d, y, c), at(z, x, y + d, c)]
    for partner in partners:
        pl.semaphore_signal(barrier, inc=1, device_id=partner, device_id_type=MESH)

    lanes = lax.broadcasted_iota(jnp.int32, (1, LANES), 1)
    sub = lax.broadcasted_iota(jnp.int32, (LANES, LANES), 0)
    lane2 = lax.broadcasted_iota(jnp.int32, (LANES, LANES), 1)
    earlier = (owner_col_ref[...] == owner_ref[...]) & (sub < lane2)
    rank = jnp.sum(earlier.astype(jnp.float32), axis=0, keepdims=True)
    live = lanes < count_ref[...]
    key = jnp.where(live, owner_ref[...].astype(jnp.float32) * 2.0 + rank, -1.0)
    scale = jnp.where(live, weight_ref[...], 0.0) * jnp.float32(0.5**0.5)
    fields = [key, start_ref[...].astype(jnp.float32), row_ref[...].astype(jnp.float32)]
    for k in range(2):
        fields += [scale * cos_ref[k : k + 1, :], scale * sin_ref[k : k + 1, :]]
    which = lax.broadcasted_iota(jnp.int32, (8, LANES), 0)
    tile = jnp.zeros((8, LANES), jnp.float32)
    for number, field in enumerate(fields):
        tile = jnp.where(which == number, field, tile)
    own_meta[...] = tile

    for k in range(2):
        ext[k, 0:64, :] = echo_ref[k * 64 : k * 64 + 64, :].astype(jnp.float32)
        halo[0, k * 4 : k * 4 + 4, :] = ext[k, 0:4, :]
    bands = []
    for ref in (tap_cos_ref, tap_sin_ref):
        taps = jnp.concatenate([ref[...], jnp.zeros((1, LANES), jnp.float32)], axis=1)
        taps = jnp.broadcast_to(taps, (LANES, 3 * LANES))
        bands.append(pltpu.roll(taps, 0, 1, stride=1, stride_axis=0).astype(jnp.bfloat16))
    band = jnp.concatenate(bands, axis=1)

    pl.semaphore_wait(barrier, len(partners))

    sends = []

    def send(src, dst, s, r, to):
        copy = pltpu.make_async_remote_copy(
            src_ref=src, dst_ref=dst, send_sem=s, recv_sem=r, device_id=to, device_id_type=MESH
        )
        copy.start()
        sends.append(copy)
        return copy

    halo_copy = send(halo.at[0], halo.at[1], halo_s, halo_r, before)
    mz = [
        send(own_meta, meta_ref.at[4 - d, x, y, c], mz_s.at[d - 1], mz_r.at[d - 1], at(z + 4 * d, x, y, c))
        for d in (1, 2, 3)
    ]
    keep_meta = pltpu.make_async_copy(own_meta, meta_ref.at[0, x, y, c], local_sem.at[0])
    keep_meta.start()
    halo_copy.wait_recv()
    inside = (rng < 7).astype(jnp.float32)
    for k in range(2):
        ext[k, 64:68, :] = halo[1, k * 4 : k * 4 + 4, :] * inside
        ext[k, 68:72, :] = jnp.zeros((4, LANES), jnp.float32)
    for k in range(2):
        whole = ext[k]
        swapped = swap_planes(whole)
        parts = [whole[2 * d : 2 * d + 64] for d in range(3)] + [swapped[2 * d : 2 * d + 64] for d in range(3)]
        windows = jnp.concatenate([part.astype(jnp.bfloat16) for part in parts], axis=1)
        filtered = lax.dot_general(windows, band, NT, preferred_element_type=jnp.float32)
        own[k] = filtered.astype(jnp.bfloat16)
    zs = [
        send(own, prof_ref.at[:, 4 - d, x, y, c], z_s.at[d - 1], z_r.at[d - 1], at(z + 4 * d, x, y, c))
        for d in (1, 2, 3)
    ]
    keep = pltpu.make_async_copy(own, prof_ref.at[:, 0, x, y, c], local_sem.at[1])
    keep.start()
    keep.wait()
    keep_meta.wait()

    near, far = pl.ds(0, 1), pl.ds(1, 3)


    def x_first(n, cut, zcut):
        first = [
            send(cut(zcut, x, y), cut(zcut, x, y), a_s.at[n, d - 1], a_r.at[n, d - 1], at(z, x + d, y, c))
            for d in (1, 2, 3)
        ]
        return n, cut, zcut, first, True

    def y_first(n, cut, zcut):
        first = [
            send(cut(zcut, x, y), cut(zcut, x, y), a_s.at[n, d - 1], a_r.at[n, d - 1], at(z, x, y + d, c))
            for d in (1, 2, 3)
        ]
        return n, cut, zcut, first, False

    def second(state):
        n, cut, zcut, first, xfirst = state
        for copy in first:
            copy.wait_recv()
        line = cut(zcut, slice(None), y) if xfirst else cut(zcut, x, slice(None))
        again = [
            send(
                line, line, b_s.at[n, d - 1], b_r.at[n, d - 1],
                at(z, x, y + d, c) if xfirst else at(z, x + d, y, c),
            )
            for d in (1, 2, 3)
        ]
        over = [send(line, line, t_s.at[n, 0], t_r.at[n, 0], twin)]
        return n, cut, zcut, again, over, xfirst

    def third(state):
        n, cut, zcut, again, over, xfirst = state
        for d, copy in zip((1, 2, 3), again):
            copy.wait_recv()
            line = (
                cut(zcut, slice(None), lax.rem(y + 4 - d, 4)) if xfirst else cut(zcut, lax.rem(x + 4 - d, 4), slice(None))
            )
            over.append(send(line, line, t_s.at[n, d], t_r.at[n, d], twin))
        return over

    def cut_of(k):
        return lambda zcut, x_, y_: prof_ref.at[k, zcut, x_, y_, c]

    def cut_meta(zcut, x_, y_):
        return meta_ref.at[zcut, x_, y_, c]

    first0 = x_first(0, cut_of(0), near)
    first1 = y_first(1, cut_of(1), near)
    for copy in mz:
        copy.wait_recv()
    first_m = x_first(4, cut_meta, pl.ds(0, 4))
    second0 = second(first0)
    second1 = second(first1)
    for copy in zs:
        copy.wait_recv()
    first2 = x_first(2, cut_of(0), far)
    first3 = y_first(3, cut_of(1), far)
    second_m = second(first_m)
    overs = third(second0) + third(second1)
    second2 = second(first2)
    second3 = second(first3)
    overs += third(second_m)
    overs += third(second2) + third(second3)
    for copy in overs:
        copy.wait_recv()
    for copy in sends:
        copy.wait_send()


def gather(echo_rows, tap_cos, tap_sin, cos, sin, start, owner, owner_col, row, weight, count):
    vmem = pl.BlockSpec(memory_space=pltpu.VMEM)
    dma = pltpu.SemaphoreType.DMA
    return pl.pallas_call(
        gather_kernel,
        out_shape=(
            jax.ShapeDtypeStruct((2, 4, 4, 4, 2, 64, LANES), jnp.bfloat16),
            jax.ShapeDtypeStruct((4, 4, 4, 2, 8, LANES), jnp.float32),
        ),
        in_specs=[vmem] * 11,
        out_specs=(pl.BlockSpec(memory_space=pl.ANY),) * 2,
        scratch_shapes=[
            pltpu.VMEM((2, 72, LANES), jnp.float32),
            pltpu.VMEM((2, 8, LANES), jnp.float32),
            pltpu.VMEM((2, 64, LANES), jnp.bfloat16),
            pltpu.VMEM((8, LANES), jnp.float32),
            dma((2,)),
            dma, dma, dma((3,)), dma((3,)), dma((3,)), dma((3,)),
            dma((5, 3)), dma((5, 3)), dma((5, 3)), dma((5, 3)), dma((5, 4)), dma((5, 4)),
        ],
        compiler_params=pltpu.CompilerParams(collective_id=0, has_side_effects=True, vmem_limit_bytes=16 << 20),
        name="gather",
    )(echo_rows, tap_cos, tap_sin, cos, sin, start, owner, owner_col, row, weight, count)


ROWS = 512


def merge_kernel(
    prof_in, meta_in, prior_ref, interp_ref, part_ref, base_ref, prof, acc, sel_i, sel_f, smem_i, smem_f, sems
):
    z, x, y, c = position()
    rng = y * 2 + c
    lanes = lax.broadcasted_iota(jnp.int32, (8, LANES), 1)
    sub = lax.broadcasted_iota(jnp.int32, (8, LANES), 0)

    keys = []
    for k in range(8):
        zo = lax.rem(z + (k // 2) + 15 - c, 16)
        keys.append(((((zo * 4 + x) * 8) + rng) * 2 + k % 2).astype(jnp.float32))

    @pl.loop(0, 8)
    def _(g):
        picked = jnp.zeros((8, LANES), jnp.float32)
        for t in range(16):
            tile = meta_in[g * 16 + t]
            key = tile[0:1, :]
            for k in range(8):
                one = jnp.sum(jnp.where(key == keys[k], tile, 0.0), axis=1, keepdims=True)
                picked = jnp.where(lanes == t * 8 + k, one, picked)
        whole = picked.astype(jnp.int32)
        start, row = whole[1:2, :], whole[2:3, :]
        lane = lanes[0:1, :]
        place = (g * 2 + lane // 64) * (2 * ROWS) + 2 * (start // LANES)
        target = lax.rem(lane, 8) // 2 * 64 + row
        ints = jnp.where(sub == 0, place, jnp.where(sub == 1, lax.rem(start, LANES), target))
        sel_i[g] = ints
        sel_f[g] = picked

    copies = [
        pltpu.make_async_copy(sel_i, smem_i, sems.at[0]),
        pltpu.make_async_copy(sel_f, smem_f, sems.at[1]),
    ]
    for copy in copies:
        copy.start()

    for k in range(2):

        @pl.loop(0, 16)
        def _(p):
            at_row = pl.multiple_of(p * (2 * ROWS) + k * ROWS, ROWS)
            prof[pl.ds(at_row, ROWS), :] = prof_in[k, p].astype(jnp.float32)

    prof[32 * ROWS : 32 * ROWS + 16, :] = jnp.zeros((16, LANES), jnp.float32)

    @pl.loop(0, 256)
    def _(i):
        acc[i] = jnp.zeros((8, LANES), jnp.float32)

    for copy in copies:
        copy.wait()

    even = lax.rem(sub, 2) == 0

    @pl.loop(0, 128)
    def _(s):
        g = s // 16
        for k in range(8):
            lane = lax.rem(s, 16) * 8 + k
            place = smem_i[g, 0, lane]
            shift = smem_i[g, 1, lane]
            target = smem_i[g, 2, lane]
            c0, s0 = smem_f[g, 3, lane], smem_f[g, 4, lane]
            c1, s1 = smem_f[g, 5, lane], smem_f[g, 6, lane]
            first = lanes >= shift
            m0 = jnp.where(first, prof[pl.ds(place, 8), :], prof[pl.ds(place + 2, 8), :])
            m1 = jnp.where(first, prof[pl.ds(place + ROWS, 8), :], prof[pl.ds(place + ROWS + 2, 8), :])
            straight = c0 * m0 + c1 * m1
            crossed = s0 * m0 + s1 * m1
            crossed = jnp.where(even, -pltpu.roll(crossed, 7, 0), pltpu.roll(crossed, 1, 0))
            acc[target] += pltpu.roll(straight + crossed, lax.rem(LANES - shift, LANES), 1)

    for o in range(4):
        part_ref[o] = acc[o * 64 : o * 64 + 64].reshape(512, LANES).astype(jnp.bfloat16)

    for i in range(8):
        fine = jnp.dot(interp_ref[...], prior_ref[i], preferred_element_type=jnp.float32)
        base_ref[pl.ds(i, 64, stride=8), :] = fine
    base_ref[...] += acc[pl.ds((1 + c) * 64, 64)].reshape(512, LANES)


def merge(prof, meta, prior, interp):
    vmem = pl.BlockSpec(memory_space=pltpu.VMEM)
    return pl.pallas_call(
        merge_kernel,
        out_shape=(
            jax.ShapeDtypeStruct((4, 512, LANES), jnp.bfloat16),
            jax.ShapeDtypeStruct((512, LANES), jnp.float32),
        ),
        in_specs=[vmem] * 4,
        out_specs=(vmem, vmem),
        scratch_shapes=[
            pltpu.VMEM((32 * ROWS + 16, LANES), jnp.float32),
            pltpu.VMEM((256, 8, LANES), jnp.float32),
            pltpu.VMEM((8, 8, LANES), jnp.int32),
            pltpu.VMEM((8, 8, LANES), jnp.float32),
            pltpu.SMEM((8, 8, LANES), jnp.int32),
            pltpu.SMEM((8, 8, LANES), jnp.float32),
            pltpu.SemaphoreType.DMA((2,)),
        ],
        compiler_params=pltpu.CompilerParams(vmem_limit_bytes=40 << 20),
        name="merge",
    )(prof, meta, prior, interp)


def exchange_kernel(part_ref, got_ref, send_sem, recv_sem):
    z, x, y, c = position()
    barrier = pltpu.get_barrier_semaphore()
    offsets = [jnp.where(c == 0, a, b) for a, b in ((-1, -2), (1, -1), (2, 1))]
    index = [jnp.where(c == 0, a, b) for a, b in ((0, 0), (2, 1), (3, 3))]
    for offset in offsets:
        pl.semaphore_signal(barrier, inc=1, device_id=at(z + offset, x, y, c), device_id_type=MESH)
        pl.semaphore_signal(barrier, inc=1, device_id=at(z - offset, x, y, c), device_id_type=MESH)
    pl.semaphore_wait(barrier, 6)
    copies = []
    for n in (2, 0, 1):
        copy = pltpu.make_async_remote_copy(
            src_ref=part_ref.at[index[n]], dst_ref=got_ref.at[n],
            send_sem=send_sem.at[n], recv_sem=recv_sem.at[n],
            device_id=at(z + offsets[n], x, y, c), device_id_type=MESH,
        )
        copy.start()
        copies.append(copy)
    for copy in copies:
        copy.wait()


def exchange(part):
    return pl.pallas_call(
        exchange_kernel,
        out_shape=jax.ShapeDtypeStruct((3, 512, LANES), jnp.bfloat16),
        in_specs=[pl.BlockSpec(memory_space=pl.ANY)],
        out_specs=pl.BlockSpec(memory_space=pl.ANY),
        scratch_shapes=[pltpu.SemaphoreType.DMA((3,)), pltpu.SemaphoreType.DMA((3,))],
        compiler_params=pltpu.CompilerParams(collective_id=1, has_side_effects=True, vmem_limit_bytes=16 << 20),
        name="exchange",
    )(part)


def on_device(
    echo, chirp_phase, rec_phase, rec_start, rec_owner, rec_row, rec_weight, rec_count, prior, interp_weight
):
    taps = chirp_phase.shape[0]
    unit = 1.0 / jnp.sqrt(jnp.float32(taps))

    def rounded(values):
        return values.astype(jnp.bfloat16).astype(jnp.float32)

    tap_cos = rounded(jnp.cos(chirp_phase) * unit)[None]
    tap_sin = rounded(jnp.sin(chirp_phase) * unit)[None]
    phases = rec_phase[0].T
    echo_rows = echo.reshape(2, 2, 32, LANES).transpose(0, 2, 1, 3).reshape(LANES, LANES)
    prof, meta = gather(
        echo_rows, tap_cos, tap_sin, rounded(jnp.cos(phases)), rounded(jnp.sin(phases)),
        rec_start, rec_owner[:, :, 0], rec_owner[0], rec_row, rec_weight, rec_count,
    )
    prior_rows = prior.reshape(32, 2, 4, LANES).transpose(2, 1, 0, 3).reshape(8, 32, LANES)
    part, base = merge(prof.reshape(2, 16, ROWS, LANES), meta.reshape(LANES, 8, LANES), prior_rows, interp_weight)
    got = exchange(part)
    total = base + got[0].astype(jnp.float32) + got[1].astype(jnp.float32) + got[2].astype(jnp.float32)
    return total.reshape(64, 4, 2, LANES).transpose(0, 2, 1, 3).reshape(64, 2, 4 * LANES)


def solution(mesh):
    placed = (
        P("pulse", None, "range"),
        P(),
        P("range", "pulse", None),
        P("range", "pulse"),
        P("range", "pulse", None),
        P("range", "pulse"),
        P("range", "pulse"),
        P("range", "pulse"),
        P("pulse", None, "range"),
        P(),
    )
    return jax.shard_map(
        on_device, mesh=mesh, in_specs=placed, out_specs=P("pulse", None, "range"), check_vma=False
    )
```

time: 258 us -> 91.4 us (0.35)
  waiting for transfers between devices: 122 us -> 0 us
  Pallas kernels: 0 us -> 82.3 us
  starting transfers between devices: 48.8 us -> 0 us
  local copies, waits for them, and re-layouts: 42.8 us -> 5.83 us
  other arithmetic: 23.8 us -> 2.2 us
  blocking collectives: 13.5 us -> 0 us
  matrix products: 3.97 us -> 0 us
    all_to_all x4 -> x0, waiting for transfers between devices: 122 us -> none  [the longest x1 96.3 us: on_device(): lax.all_to_all(outgoing, 'pulse', split_axis=0, concat_axis=0, tiled=True)]
    pallas_call x0 -> x3, Pallas kernels: none -> 82.3 us  [the longest x1 45.6 us: gather(): pl.pallas_call(gather_kernel, out_shape=(jax.ShapeDtypeStruct((2, 4, 4, 4...]
    all_to_all x4 -> x0, starting transfers between devices: 40 us -> none  [the longest x1 14.8 us: on_device(): lax.all_to_all(outgoing, 'pulse', split_axis=0, concat_axis=0, tiled=True)]
    slice x27 -> x0, local copies, waits for them, and re-layouts: 17.1 us -> none  [the longest x18 15.4 us: cut_windows(): paired[..., step_size:]]
    select_n x22 -> x0, other arithmetic: 16.4 us -> none  [the longest x18 16.4 us: cut_windows(): paired = jnp.where(chosen, moved, paired)]
    all_gather x1 -> x0, blocking collectives: 13.5 us -> none  [on_device(): lax.all_gather(compress(echo, tail_rim, filter_matrix), 'range', axis=2,...]
    ppermute x1 -> x0, starting transfers between devices: 8.77 us -> none  [shifted(): return lax.ppermute(block, axis, route)]
    all_to_all x5 -> x0, local copies, waits for them, and re-layouts: 7.48 us -> none  [the longest x1 3.76 us: on_device(): lax.all_to_all(lax.all_to_all(outgoing, 'pulse', split_axis=0, concat_axi...]
  transfers between devices with their start and end apart: 5 -> 0, of which waited for: 3 -> 0; matrix products, arithmetic and copies ran while one was open for 24% -> 0% of each run, Pallas kernels for 0% -> 0%
where the time goes in v1:
time: 91.4 us; the launch traced here: 91 us
  Pallas kernels  82.3 us (90%)
  local copies, waits for them, and re-layouts  5.83 us (6%)
  other arithmetic  2.2 us (2%)
    pallas_call x1, Pallas kernels, gather(): pl.pallas_call(gather_kernel, out_shape=(jax.ShapeDtypeStruct((2, 4, 4, 4...  45.6 us
    pallas_call x1, Pallas kernels, merge(): pl.pallas_call(merge_kernel, out_shape=(jax.ShapeDtypeStruct((4, 512, LAN...  23.9 us
    pallas_call x1, Pallas kernels, exchange(): pl.pallas_call(exchange_kernel, out_shape=jax.ShapeDtypeStruct((3, 512, L...  12.7 us
    unnamed x11, local copies, waits for them, and re-layouts  4.16 us

profile of v1, /device:TPU:1, one launch (start us, length us, event | category | flops | bytes accessed | tf_op | source)
XLA Modules:
  0.0 91.0 jit_solution(1915940772664372515)
XLA Ops:
  0.7 0.7 fusion.1
  1.4 0.7 convert_bitcast_fusion
  2.1 0.8 copy.14.interp_ref
  2.9 0.9 reshape.42
  3.8 0.8 copy.12.owner_col_ref
  4.6 0.0 copy-start
  4.6 0.8 copy-done
  5.3 0.0 copy-start.1
  5.3 0.7 copy-done.1
  6.0 0.0 copy-start.2
  6.0 0.7 copy-done.2
  6.6 0.0 copy-start.3
  6.6 0.7 copy-done.3
  7.3 0.0 copy-start.4
  7.3 0.7 copy-done.4
  7.9 45.6 %gather.1 = (bf16[2,4,4,4,2,64,128]{6,5,4,3,2,1,0:T(8,128)(2,1)S(1)}, f32[4,4,4,2,8,128]{5,4,3,2,1,0:T(8,128)S(1)}) custom-call(bf16[128,128]{1,0:T(8,128)(2,1)S(1)} %bitcast.45, f32[1,256]{1,0:T(1,128)S(1)} %bitcast.47, f32[1,256]{1,0:T(1,128)S(1)} %bitcast.46, f32[2,128]{1,0:T(2,128)S(1)} %get-tuple-element.14.cos_ref, ...), custom_call_target="tpu_custom_call" | custom-call | tf_op jit(solution)/shard_map/gather/pallas_call | solution.py:190
  53.6 23.9 %merge.1 = (bf16[4,512,128]{2,1,0:T(8,128)(2,1)S(1)}, f32[512,128]{1,0:T(8,128)S(1)}) custom-call(bf16[2,16,512,128]{3,2,1,0:T(8,128)(2,1)S(1)} %bitcast.42, f32[128,8,128]{2,1,0:T(8,128)S(1)} %bitcast.43, bf16[8,32,128]{2,1,0:T(8,128)(2,1)S(1)} %bitcast.44, bf16[64,32]{1,0:T(8,128)(2,1)S(1)} %copy.14.interp_ref), custom_call_target="tpu_custom_call" | custom-call | tf_op jit(solution)/shard_map/merge/pallas_call | solution.py:300
  77.5 12.7 %exchange.1 = bf16[3,512,128]{2,1,0:T(8,128)(2,1)S(1)} custom-call(bf16[4,512,128]{2,1,0:T(8,128)(2,1)S(1)} %get-tuple-element.12.part_ref), custom_call_target="tpu_custom_call" | custom-call | tf_op jit(solution)/shard_map/exchange/pallas_call | solution.py:345
  90.2 0.8 convert_add_fusion
  (1 shorter events, 0.0 us)
Async XLA Ops:
  4.6 0.8 copy-start
  5.3 0.7 copy-start.1
  6.0 0.7 copy-start.2
  6.6 0.7 copy-start.3
  7.3 0.7 copy-start.4

commit v2 on v0

v2 whole, which is shorter than its diff:
```python
import jax
import jax.numpy as jnp
from jax import lax
from jax.experimental import pallas as pl
from jax.experimental.pallas import tpu as pltpu
from jax.sharding import PartitionSpec as P

MESH = pl.DeviceIdType.MESH
LANES = 128
ROWS = 512
NT = (((1,), (1,)), ((), ()))
TN = (((0,), (0,)), ((), ()))
INPUTS = 9


def position():
    pulse, rng = lax.axis_index("pulse"), lax.axis_index("range")
    return pulse // 4, lax.rem(pulse, 4), rng // 2, lax.rem(rng, 2)


def at(z, x, y, c):
    return (lax.rem(z + 16, 16) * 4 + lax.rem(x + 4, 4), lax.rem(y + 4, 4) * 2 + c)


def swap_planes(rows):
    count = rows.shape[0]
    even = lax.rem(lax.broadcasted_iota(jnp.int32, rows.shape, 0), 2) == 0
    return jnp.where(even, pltpu.roll(rows, count - 1, 0), -pltpu.roll(rows, 1, 0))


def describe(phase, start, owner, row, weight, count):
    shape = (LANES, LANES)
    lanes = lax.broadcasted_iota(jnp.int32, (1, LANES), 1)
    number = owner[...].astype(jnp.float32)
    across = jnp.broadcast_to(number, shape)
    earlier = lax.broadcasted_iota(jnp.int32, shape, 0) < lax.broadcasted_iota(jnp.int32, shape, 1)
    same = (across.T == across) & earlier
    rank = jnp.sum(same.astype(jnp.float32), axis=0, keepdims=True)
    live = lanes < count[0, 0]
    key = jnp.where(live, number * 2.0 + rank, -1.0)
    scale = jnp.where(live, weight[...], 0.0) * jnp.float32(0.5**0.5)
    fields = [key] + [
        field.astype(jnp.float32) for field in (start[...] // LANES, lax.rem(start[...], LANES), row[...])
    ]
    for k in range(2):
        for turn in (jnp.cos, jnp.sin):
            fields.append(scale * turn(phase[k : k + 1, :]).astype(jnp.bfloat16).astype(jnp.float32))
    which = lax.broadcasted_iota(jnp.int32, (8, LANES), 0)
    tile = jnp.zeros((8, LANES), jnp.float32)
    for place, field in enumerate(fields):
        tile = jnp.where(which == place, field, tile)
    return tile


def tap_band(chirp):
    bands = []
    for turn in (jnp.cos, jnp.sin):
        taps = turn(chirp[...]) * jnp.float32(1 / 16)
        taps = jnp.concatenate([taps, jnp.zeros((1, LANES), jnp.float32)], axis=1)
        taps = jnp.broadcast_to(taps, (LANES, 3 * LANES))
        bands.append(pltpu.roll(taps, 0, 1, stride=1, stride_axis=0).astype(jnp.bfloat16))
    return jnp.concatenate(bands, axis=1)


def kernel(*refs):
    given, count, out_ref, held = refs[:INPUTS], refs[INPUTS], refs[INPUTS + 1], refs[INPUTS + 2 : 2 * INPUTS + 2]
    echo, chirp, phase, start, owner, row, weight, prior, interp = held
    (
        in_sem, ext, halo, raw, meta, prof, slots, rows, codes, sel, smem, stage, part, got, coarse, base, smem_sem,
        halo_s, halo_r, z_s, z_r, mz_s, mz_r, a_s, a_r, b_s, b_r, t_s, t_r, e_s, e_r,
    ) = refs[2 * INPUTS + 2 :]
    z, x, y, c = position()
    rng = y * 2 + c
    pulse = lax.axis_index("pulse")
    twin = at(z, x, y, 1 - c)
    before, after = (pulse, lax.rem(rng + 7, 8)), (pulse, lax.rem(rng + 1, 8))

    loads = [pltpu.make_async_copy(src, dst, in_sem.at[n]) for n, (src, dst) in enumerate(zip(given, held))]
    for load in loads:
        load.start()
    barrier = pltpu.get_barrier_semaphore()
    partners = [twin, before, after]
    for d in (1, 2, 3):
        partners += [at(z + 4 * d, x, y, c), at(z, x + d, y, c), at(z, x, y + d, c)]
    for d in (-2, -1, 1, 2):
        partners.append(at(z + d, x, y, c))
    for partner in partners:
        pl.semaphore_signal(barrier, inc=1, device_id=partner, device_id_type=MESH)
    for load in loads:
        load.wait()

    meta[0, x, y, c] = describe(phase, start, owner, row, weight, count)
    for k in range(2):
        ext[k, 0:64, :] = echo[k * 64 : k * 64 + 64, :].astype(jnp.float32)
        halo[0, k * 4 : k * 4 + 4, :] = ext[k, 0:4, :]
    band = tap_band(chirp)
    pl.semaphore_wait(barrier, len(partners))

    sends = []

    def send(src, dst, s, r, to):
        copy = pltpu.make_async_remote_copy(
            src_ref=src, dst_ref=dst, send_sem=s, recv_sem=r, device_id=to, device_id_type=MESH
        )
        copy.start()
        sends.append(copy)
        return copy

    def arrived(copies):
        for copy in copies:
            copy.wait_recv()

    halo_copy = send(halo.at[0], halo.at[1], halo_s, halo_r, before)
    mz = {
        d: send(
            meta.at[0, x, y, c], meta.at[4 - d, x, y, c], mz_s.at[d - 1], mz_r.at[d - 1], at(z + 4 * d, x, y, c)
        )
        for d in (2, 1, 3)
    }
    arrived([halo_copy])
    inside = (rng < 7).astype(jnp.float32)
    for k in range(2):
        ext[k, 64:68, :] = halo[1, k * 4 : k * 4 + 4, :] * inside
        ext[k, 68:72, :] = jnp.zeros((4, LANES), jnp.float32)
    for k in range(2):
        whole = ext[k]
        swapped = swap_planes(whole)
        parts = [whole[2 * d : 2 * d + 64] for d in range(3)] + [swapped[2 * d : 2 * d + 64] for d in range(3)]
        windows = jnp.concatenate([piece.astype(jnp.bfloat16) for piece in parts], axis=1)
        filtered = lax.dot_general(windows, band, NT, preferred_element_type=jnp.float32)
        raw[0, k, x, y, c] = filtered.astype(jnp.bfloat16)
    zs = {
        d: send(
            raw.at[0, :, x, y, c], raw.at[4 - d, :, x, y, c], z_s.at[d - 1], z_r.at[d - 1], at(z + 4 * d, x, y, c)
        )
        for d in (2, 1, 3)
    }

    def spread(n, cut, x_first):
        here = cut(x, y)
        return [
            send(
                here, here, a_s.at[n, d - 1], a_r.at[n, d - 1],
                at(z, x + d, y, c) if x_first else at(z, x, y + d, c),
            )
            for d in (1, 3, 2)
        ]

    def spread_line(n, cut, x_first):
        line = cut(slice(None), y) if x_first else cut(x, slice(None))
        again = {
            d: send(
                line, line, b_s.at[n, d - 1], b_r.at[n, d - 1],
                at(z, x, y + d, c) if x_first else at(z, x + d, y, c),
            )
            for d in (1, 3, 2)
        }
        return again, [send(line, line, t_s.at[n, 0], t_r.at[n, 0], twin)]

    def to_twin(n, cut, x_first, state):
        again, over = state
        for d, copy in again.items():
            copy.wait_recv()
            line = cut(slice(None), lax.rem(y + 4 - d, 4)) if x_first else cut(lax.rem(x + 4 - d, 4), slice(None))
            over.append(send(line, line, t_s.at[n, d], t_r.at[n, d], twin))
        return over

    def cut_of(zrel, k):
        return lambda x_, y_: raw.at[zrel, k, x_, y_, c]

    def cut_meta(x_, y_):
        return meta.at[:, x_, y_, c]

    class PlaneSet:
        def __init__(self, zrel):
            self.kinds = [(zrel * 2 + k, cut_of(zrel, k), k == 0) for k in range(2)]

        def first(self):
            self.along = [spread(*kind) for kind in self.kinds]

        def second(self):
            self.states = []
            for kind, along in zip(self.kinds, self.along):
                arrived(along)
                self.states.append(spread_line(*kind))

        def third(self):
            self.over = []
            for kind, state in zip(self.kinds, self.states):
                self.over += to_twin(*kind, state)

    planes = [PlaneSet(zrel) for zrel in range(4)]
    meta_kind = (8, cut_meta, True)

    lanes = lax.broadcasted_iota(jnp.int32, (8, LANES), 1)
    lane1 = lanes[0:1, :]
    sub = lax.broadcasted_iota(jnp.int32, (8, LANES), 0)
    even = lax.rem(sub, 2) == 0
    keys = []
    for k in range(8):
        zo = lax.rem(z + (k // 2) + 15 - c, 16)
        keys.append(((((zo * 4 + x) * 8) + rng) * 2 + k % 2).astype(jnp.float32))

    def select():
        @pl.loop(0, 8)
        def _(g):
            found = [jnp.full((1, LANES), -1.0, jnp.float32) for _ in range(4)]
            for t in range(16):
                tile = meta[g // 2, lax.rem(g, 2) * 2 + t // 8, t % 8 // 2, t % 2]
                key = tile[0:1, :]
                code = tile[1:2, :] * 16384.0 + tile[2:3, :] * 128.0
                tile = jnp.where(sub == 0, code, tile)
                line = jnp.zeros((1, LANES), jnp.float32)
                for k in range(8):
                    one = jnp.sum(jnp.where(key == keys[k], tile, 0.0), axis=1, keepdims=True)
                    one = jnp.broadcast_to(one, (8, LANES))
                    slots[(g * 16 + t) * 8 + k] = one
                    line = jnp.where(lane1 == k, one[0:1, :], line)
                    found[k // 2] = jnp.where(lane1 == t * 2 + k % 2, one[3:4, :], found[k // 2])
                codes[pl.ds(g * 16 + t, 1), :] = line
            for o in range(4):
                rows[g, o : o + 1, :] = found[o]

        sel[...] = codes[...].astype(jnp.int32)
        copy = pltpu.make_async_copy(sel, smem, smem_sem)
        copy.start()
        copy.wait()

    def form(zrel):
        arrived(planes[zrel].over)

        @pl.loop(0, 4)
        def _(p):
            base_row = (zrel * 4 + p) * (2 * ROWS)
            for k in range(2):
                at_row = pl.multiple_of(base_row + k * ROWS, ROWS)
                prof[pl.ds(at_row, ROWS), :] = raw[zrel, k, p].reshape(ROWS, LANES).astype(jnp.float32)

        @pl.loop(zrel * 4, zrel * 4 + 4)
        def _(p):
            made = []
            for k in range(64):
                s = p * 8 + k // 8
                code = smem[s, k % 8]
                place = p * (2 * ROWS) + ((code >> 13) & 510)
                turn = (code >> 7) & (LANES - 1)
                slot = slots.at[s * 8 + k % 8]
                first = lanes.astype(jnp.float32) >= slot[2:3, :]
                c0, s0, c1, s1 = (slot[i : i + 1, :] for i in range(4, 8))
                m0 = jnp.where(first, prof[pl.ds(place, 8), :], prof[pl.ds(place + 2, 8), :])
                m1 = jnp.where(first, prof[pl.ds(place + ROWS, 8), :], prof[pl.ds(place + ROWS + 2, 8), :])
                straight = c0 * m0 + c1 * m1
                crossed = s0 * m0 + s1 * m1
                crossed = jnp.where(even, -pltpu.roll(crossed, 7, 0), pltpu.roll(crossed, 1, 0))
                made.append(pltpu.roll(straight + crossed, (LANES - turn) & (LANES - 1), 1))
            for k, record in enumerate(made):
                s = p * 8 + k // 8
                stage[k % 8 // 2, pl.ds(s * 2 + k % 2, 8, stride=256), :] = record

    prof[32 * ROWS : 32 * ROWS + 16, :] = jnp.zeros((16, LANES), jnp.float32)
    planes[0].first()
    arrived(mz.values())
    along = spread(*meta_kind)
    planes[0].second()
    arrived(along)
    meta_state = spread_line(*meta_kind)
    arrived([zs[1]])
    planes[3].first()
    arrived([zs[3]])
    planes[1].first()
    over = to_twin(*meta_kind, meta_state)
    planes[0].third()
    planes[3].second()
    planes[1].second()
    arrived(over)
    select()
    arrived([zs[2]])
    planes[2].first()
    form(0)
    planes[2].second()
    planes[3].third()
    planes[1].third()
    form(3)
    planes[2].third()
    form(1)
    form(2)

    def total(o, i, marks):
        records = stage[o, i * 256 : i * 256 + 256, :].astype(jnp.bfloat16)
        return jnp.dot(marks, records, preferred_element_type=jnp.float32)

    def marks_of(o):
        row_of = jnp.concatenate([rows[g, pl.ds(o, 1), 0:32] for g in range(8)], axis=1)
        level = lax.broadcasted_iota(jnp.int32, (64, 256), 0).astype(jnp.float32)
        return (level == row_of).astype(jnp.bfloat16)

    parts_sent = []
    for n, (low, high) in enumerate(((3, 0), (0, 1), (2, 3))):
        o = jnp.where(c == 0, low, high)
        marks = marks_of(o)
        for i in range(8):
            part[n, i * 64 : i * 64 + 64, :] = total(o, i, marks).astype(jnp.bfloat16)
        parts_sent.append(send(part.at[n], got.at[n], e_s.at[n], e_r.at[n], at(z + o - 1 - c, x, y, c)))

    coarse[...] = prior[...].astype(jnp.float32)
    marks = marks_of(1 + c)
    for i in range(8):
        piece = coarse[pl.ds(i, 32, stride=8), :].astype(jnp.bfloat16)
        fine = lax.dot_general(interp[...], piece, TN, preferred_element_type=jnp.float32)
        base[i * 64 : i * 64 + 64, :] = fine + total(1 + c, i, marks)
    arrived(parts_sent)
    for i in range(8):
        whole = base[i * 64 : i * 64 + 64, :]
        for n in range(3):
            whole = whole + got[n, i * 64 : i * 64 + 64, :].astype(jnp.float32)
        out_ref[pl.ds(i, 64, stride=8), :] = whole
    for copy in sends:
        copy.wait_send()


def merged(*inputs):
    anywhere = pl.BlockSpec(memory_space=pl.ANY)
    dma = pltpu.SemaphoreType.DMA
    f32, bf16 = jnp.float32, jnp.bfloat16
    return pl.pallas_call(
        kernel,
        out_shape=jax.ShapeDtypeStruct((512, LANES), f32),
        in_specs=[anywhere] * INPUTS + [pl.BlockSpec(memory_space=pltpu.SMEM)],
        out_specs=pl.BlockSpec(memory_space=pltpu.VMEM),
        scratch_shapes=[pltpu.VMEM(a.shape, a.dtype) for a in inputs[:INPUTS]]
        + [
            dma((INPUTS,)),
            pltpu.VMEM((2, 72, LANES), f32),
            pltpu.VMEM((2, 8, LANES), f32),
            pltpu.VMEM((4, 2, 4, 4, 2, 64, LANES), bf16),
            pltpu.VMEM((4, 4, 4, 2, 8, LANES), f32),
            pltpu.VMEM((32 * ROWS + 16, LANES), f32),
            pltpu.VMEM((1024, 8, LANES), f32),
            pltpu.VMEM((8, 8, LANES), f32),
            pltpu.VMEM((LANES, LANES), f32),
            pltpu.VMEM((LANES, LANES), jnp.int32),
            pltpu.SMEM((LANES, LANES), jnp.int32),
            pltpu.VMEM((4, 2048, LANES), f32),
            pltpu.VMEM((3, 512, LANES), bf16),
            pltpu.VMEM((3, 512, LANES), bf16),
            pltpu.VMEM((256, LANES), f32),
            pltpu.VMEM((512, LANES), f32),
            dma,
            dma, dma, dma((3,)), dma((3,)), dma((3,)), dma((3,)),
            dma((9, 3)), dma((9, 3)), dma((9, 3)), dma((9, 3)), dma((9, 4)), dma((9, 4)),
            dma((3,)), dma((3,)),
        ],
        compiler_params=pltpu.CompilerParams(collective_id=0, has_side_effects=True, vmem_limit_bytes=56 << 20),
        name="merged",
    )(*inputs)


def on_device(
    echo, chirp_phase, rec_phase, rec_start, rec_owner, rec_row, rec_weight, rec_count, prior, interp_weight
):
    def by_block(array):
        count, blocks = array.shape[0], array.shape[2] // LANES
        array = array.reshape(count, 2, blocks, LANES).transpose(0, 2, 1, 3)
        return array.reshape(count * blocks * 2, LANES)

    tiles = merged(
        by_block(echo), chirp_phase[None], rec_phase[0].T, rec_start, rec_owner[:, :, 0], rec_row, rec_weight,
        by_block(prior), interp_weight.T, rec_count,
    )
    return tiles.reshape(64, 4, 2, LANES).transpose(0, 2, 1, 3).reshape(64, 2, 4 * LANES)


def solution(mesh):
    placed = (
        P("pulse", None, "range"),
        P(),
        P("range", "pulse", None),
        P("range", "pulse"),
        P("range", "pulse", None),
        P("range", "pulse"),
        P("range", "pulse"),
        P("range", "pulse"),
        P("pulse", None, "range"),
        P(),
    )
    return jax.shard_map(
        on_device, mesh=mesh, in_specs=placed, out_specs=P("pulse", None, "range"), check_vma=False
    )
```

time: 258 us -> 63 us (0.24)
  waiting for transfers between devices: 122 us -> 0 us
  Pallas kernels: 0 us -> 59.6 us
  starting transfers between devices: 48.8 us -> 0 us
  local copies, waits for them, and re-layouts: 42.8 us -> 1.67 us
  other arithmetic: 23.8 us -> 0 us
  blocking collectives: 13.5 us -> 0 us
  matrix products: 3.97 us -> 0 us
    all_to_all x4 -> x0, waiting for transfers between devices: 122 us -> none  [the longest x1 96.3 us: on_device(): lax.all_to_all(outgoing, 'pulse', split_axis=0, concat_axis=0, tiled=True)]
    pallas_call x0 -> x1, Pallas kernels: none -> 59.6 us  [merged(): pl.pallas_call(kernel, out_shape=jax.ShapeDtypeStruct((512, LANES), f32),...]
    all_to_all x4 -> x0, starting transfers between devices: 40 us -> none  [the longest x1 14.8 us: on_device(): lax.all_to_all(outgoing, 'pulse', split_axis=0, concat_axis=0, tiled=True)]
    slice x27 -> x0, local copies, waits for them, and re-layouts: 17.1 us -> none  [the longest x18 15.4 us: cut_windows(): paired[..., step_size:]]
    select_n x22 -> x0, other arithmetic: 16.4 us -> none  [the longest x18 16.4 us: cut_windows(): paired = jnp.where(chosen, moved, paired)]
    all_gather x1 -> x0, blocking collectives: 13.5 us -> none  [on_device(): lax.all_gather(compress(echo, tail_rim, filter_matrix), 'range', axis=2,...]
    ppermute x1 -> x0, starting transfers between devices: 8.77 us -> none  [shifted(): return lax.ppermute(block, axis, route)]
    all_to_all x5 -> x0, local copies, waits for them, and re-layouts: 7.48 us -> none  [the longest x1 3.76 us: on_device(): lax.all_to_all(lax.all_to_all(outgoing, 'pulse', split_axis=0, concat_axi...]
  transfers between devices with their start and end apart: 5 -> 0, of which waited for: 3 -> 0; matrix products, arithmetic and copies ran while one was open for 24% -> 0% of each run, Pallas kernels for 0% -> 0%
where the time goes in v2:
time: 63 us; the launch traced here: 61.9 us
  Pallas kernels  59.6 us (95%)
  local copies, waits for them, and re-layouts  1.67 us (3%)
  between operations  0.66 us (1%)
    pallas_call x1, Pallas kernels, merged(): pl.pallas_call(kernel, out_shape=jax.ShapeDtypeStruct((512, LANES), f32),...  59.6 us
    unnamed x1, local copies, waits for them, and re-layouts  1.67 us

profile of v2, /device:TPU:1, one launch (start us, length us, event | category | flops | bytes accessed | tf_op | source)
XLA Modules:
  0.0 61.9 jit_solution(2464525698510224221)
XLA Ops:
  0.7 59.6 %merged.1 = f32[512,128]{1,0:T(8,128)} custom-call(bf16[128,128]{1,0:T(8,128)(2,1)} %bitcast.23, f32[1,256]{1,0:T(1,128)} %bitcast.25, f32[2,128]{1,0:T(2,128)} %bitcast.26, s32[1,128]{1,0:T(1,128)} %refs_3_.1, s32[1,128]{1,0:T(1,128)} %bitcast.27, s32[1,128]{1,0:T(1,128)} %refs_5_.1, f32[1,128]{1,0:T(1,128)} %refs_6_.1, bf16[256,128]{1,0:T(8,128)(2,1)} %bitcast.22, ...), custom_call_target="tpu_custom_call" | custom-call | tf_op jit(solution)/shard_map/merged/pallas_call | solution.py:325
  60.2 1.7 %copy.16 = f32[64,2,512]{2,1,0:T(2,128)} copy(f32[64,2,512]{2,1,0:T(2,128)} %bitcast.21) | data formatting | bytes 524288

commit v3 on v2

--- a/solution.py
+++ b/solution.py
@@ -259,26 +259,22 @@
 
     prof[32 * ROWS : 32 * ROWS + 16, :] = jnp.zeros((16, LANES), jnp.float32)
     planes[0].first()
+    planes[0].second()
     arrived(mz.values())
     along = spread(*meta_kind)
-    planes[0].second()
+    for d in (1, 3, 2):
+        arrived([zs[d]])
+        planes[4 - d].first()
     arrived(along)
     meta_state = spread_line(*meta_kind)
-    arrived([zs[1]])
-    planes[3].first()
-    arrived([zs[3]])
-    planes[1].first()
+    planes[0].third()
+    for zrel in (3, 1, 2):
+        planes[zrel].second()
     over = to_twin(*meta_kind, meta_state)
-    planes[0].third()
-    planes[3].second()
-    planes[1].second()
     arrived(over)
     select()
-    arrived([zs[2]])
-    planes[2].first()
+    planes[3].third()
     form(0)
-    planes[2].second()
-    planes[3].third()
     planes[1].third()
     form(3)
     planes[2].third()

time: 63 us -> 58.8 us (0.933); the launches traced: 61.9 us -> 58.6 us
  Pallas kernels: 59.6 us -> 56.3 us
    pallas_call x1, Pallas kernels: 59.6 us -> 56.3 us  [merged(): pl.pallas_call(kernel, out_shape=jax.ShapeDtypeStruct((512, LANES), f32),...]
where the time goes in v3:
time: 58.8 us; the launch traced here: 58.6 us
  Pallas kernels  56.3 us (96%)
  local copies, waits for them, and re-layouts  1.67 us (3%)
  between operations  0.66 us (1%)
    pallas_call x1, Pallas kernels, merged(): pl.pallas_call(kernel, out_shape=jax.ShapeDtypeStruct((512, LANES), f32),...  56.3 us
    unnamed x1, local copies, waits for them, and re-layouts  1.67 us

profile of v3, /device:TPU:1, one launch (start us, length us, event | category | flops | bytes accessed | tf_op | source)
XLA Modules:
  0.0 58.6 jit_solution(794171910270065656)
XLA Ops:
  0.7 56.3 %merged.1 = f32[512,128]{1,0:T(8,128)} custom-call(bf16[128,128]{1,0:T(8,128)(2,1)} %bitcast.23, f32[1,256]{1,0:T(1,128)} %bitcast.25, f32[2,128]{1,0:T(2,128)} %bitcast.26, s32[1,128]{1,0:T(1,128)} %refs_3_.1, s32[1,128]{1,0:T(1,128)} %bitcast.27, s32[1,128]{1,0:T(1,128)} %refs_5_.1, f32[1,128]{1,0:T(1,128)} %refs_6_.1, bf16[256,128]{1,0:T(8,128)(2,1)} %bitcast.22, ...), custom_call_target="tpu_custom_call" | custom-call | tf_op jit(solution)/shard_map/merged/pallas_call | solution.py:321
  56.9 1.7 %copy.16 = f32[64,2,512]{2,1,0:T(2,128)} copy(f32[64,2,512]{2,1,0:T(2,128)} %bitcast.21) | data formatting | bytes 524288

commit v4 on v3

--- a/solution.py
+++ b/solution.py
@@ -168,8 +168,8 @@
     def cut_of(zrel, k):
         return lambda x_, y_: raw.at[zrel, k, x_, y_, c]
 
-    def cut_meta(x_, y_):
-        return meta.at[:, x_, y_, c]
+    def cut_meta(half):
+        return lambda x_, y_: meta.at[pl.ds(2 * half, 2), x_, y_, c]
 
     class PlaneSet:
         def __init__(self, zrel):
@@ -190,7 +190,7 @@
                 self.over += to_twin(*kind, state)
 
     planes = [PlaneSet(zrel) for zrel in range(4)]
-    meta_kind = (8, cut_meta, True)
+    meta_kinds = [(8 + half, cut_meta(half), half == 0) for half in range(2)]
 
     lanes = lax.broadcasted_iota(jnp.int32, (8, LANES), 1)
     lane1 = lanes[0:1, :]
@@ -261,17 +261,20 @@
     planes[0].first()
     planes[0].second()
     arrived(mz.values())
-    along = spread(*meta_kind)
+    alongs = [spread(*kind) for kind in meta_kinds]
     for d in (1, 3, 2):
         arrived([zs[d]])
         planes[4 - d].first()
-    arrived(along)
-    meta_state = spread_line(*meta_kind)
+    meta_states = []
+    for kind, along in zip(meta_kinds, alongs):
+        arrived(along)
+        meta_states.append(spread_line(*kind))
     planes[0].third()
     for zrel in (3, 1, 2):
         planes[zrel].second()
-    over = to_twin(*meta_kind, meta_state)
-    arrived(over)
+    overs = [to_twin(*kind, state) for kind, state in zip(meta_kinds, meta_states)]
+    for over in overs:
+        arrived(over)
     select()
     planes[3].third()
     form(0)
@@ -343,7 +346,7 @@
             pltpu.VMEM((512, LANES), f32),
             dma,
             dma, dma, dma((3,)), dma((3,)), dma((3,)), dma((3,)),
-            dma((9, 3)), dma((9, 3)), dma((9, 3)), dma((9, 3)), dma((9, 4)), dma((9, 4)),
+            dma((10, 3)), dma((10, 3)), dma((10, 3)), dma((10, 3)), dma((10, 4)), dma((10, 4)),
             dma((3,)), dma((3,)),
         ],
         compiler_params=pltpu.CompilerParams(collective_id=0, has_side_effects=True, vmem_limit_bytes=56 << 20),

time: 58.8 us -> 57.9 us (0.985)
  Pallas kernels: 56.3 us -> 55.3 us
    pallas_call x1, Pallas kernels: 56.3 us -> 55.3 us  [merged(): pl.pallas_call(kernel, out_shape=jax.ShapeDtypeStruct((512, LANES), f32),...]
where the time goes in v4:
time: 57.9 us; the launch traced here: 57.7 us
  Pallas kernels  55.3 us (96%)
  local copies, waits for them, and re-layouts  1.67 us (3%)
  between operations  0.66 us (1%)
    pallas_call x1, Pallas kernels, merged(): pl.pallas_call(kernel, out_shape=jax.ShapeDtypeStruct((512, LANES), f32),...  55.3 us
    unnamed x1, local copies, waits for them, and re-layouts  1.67 us

profile of v4, /device:TPU:1, one launch (start us, length us, event | category | flops | bytes accessed | tf_op | source)
XLA Modules:
  0.0 57.7 jit_solution(2029920443311973311)
XLA Ops:
  0.7 55.3 %merged.1 = f32[512,128]{1,0:T(8,128)} custom-call(bf16[128,128]{1,0:T(8,128)(2,1)} %bitcast.23, f32[1,256]{1,0:T(1,128)} %bitcast.25, f32[2,128]{1,0:T(2,128)} %bitcast.26, s32[1,128]{1,0:T(1,128)} %refs_3_.1, s32[1,128]{1,0:T(1,128)} %bitcast.27, s32[1,128]{1,0:T(1,128)} %refs_5_.1, f32[1,128]{1,0:T(1,128)} %refs_6_.1, bf16[256,128]{1,0:T(8,128)(2,1)} %bitcast.22, ...), custom_call_target="tpu_custom_call" | custom-call | tf_op jit(solution)/shard_map/merged/pallas_call | solution.py:324
  56.0 1.7 %copy.16 = f32[64,2,512]{2,1,0:T(2,128)} copy(f32[64,2,512]{2,1,0:T(2,128)} %bitcast.21) | data formatting | bytes 524288
